TPU v7x, 512 devices: a whole 4x8x8 slice. The times are simulated.
512 devices in a mesh: dp: 32 (over x, y_lo, core), vocab: 16 (over z, y_hi).
Axes of the slice: x: 4, y: 8 (y_hi: 2, y_lo: 4; y = y_hi * 4 + y_lo), z: 8, core: 2. Of those that a mesh axis runs over, the one named last changes fastest.
Arguments:
- hidden: bfloat16 [7168, 4096], P('dp'), may hold values from -6 to 6
- head_weight: bfloat16 [4096, 16384], P('dp', 'vocab'), may hold values from -0.09375 to 0.09375
- head_bias: float32 [16384], P('vocab'), may hold values from -1 to 1
- lengths: int32 [64, 2], P('dp'), may hold values from 1 to 80, as said below
- positives: int32 [64], P('dp'), may hold values from 0 to 63, each once
Outputs:
- hidden_grad: bfloat16 [7168, 4096], P(('dp', 'vocab'))
Inputs may be any that keep to these rules, and one draw needn't show every extreme that they name: `lengths`: query counts are at most 32, passage counts at most 80; the first slots of each are used.
All inputs are finite; a program needn't handle non-finite values.
Results may differ from a plain program's by a relative error of at most 0.0064.
Values may be sent and summed in bfloat16 or wider, within the bound.
A program may use at most 64 MiB of HBM per device.

v0:
```python
import jax
import jax.numpy as jnp
from jax import lax
from jax.sharding import PartitionSpec as P

QLEN = 32


POOL_TEMP = 0.25
SCORE_TEMP = 0.01
LOSS_SCALE = 65536.0


def row_mask(lengths, rows_pair):
    position = lax.broadcasted_iota(jnp.int32, (1, rows_pair), 1)
    is_query = position < QLEN
    offset = jnp.where(is_query, position, position - QLEN)
    limit_len = jnp.where(is_query, lengths[:, 0:1], lengths[:, 1:2])
    return (offset < limit_len).astype(jnp.float32)


def pool_terms(logits, token_mask):
    softened = jax.nn.softplus(logits)
    boosted = token_mask[:, :, None] * jnp.exp(jnp.log1p(softened) / POOL_TEMP)
    return (softened, boosted)


def pooled_vectors(boosted, lengths):
    query_sum = jnp.sum(boosted[:, :QLEN], axis=1)
    passage_sum = jnp.sum(boosted[:, QLEN:], axis=1)
    query_vec = POOL_TEMP * jnp.log(query_sum / lengths[:, 0:1].astype(jnp.float32))
    passage_vec = POOL_TEMP * jnp.log(passage_sum / lengths[:, 1:2].astype(jnp.float32))
    return (query_vec, passage_vec, query_sum, passage_sum)


def score_grads(scores, positives, pair_count):
    row_max = jnp.max(scores, axis=1, keepdims=True)
    shifted = jnp.exp(scores - row_max)
    softmax_out = shifted / jnp.sum(shifted, axis=1, keepdims=True)
    target = (positives[:, None] == lax.broadcasted_iota(jnp.int32, (1, pair_count), 1)).astype(
        jnp.float32
    )
    return LOSS_SCALE * (softmax_out - target)


def logit_grads(logits, softened, boosted, query_sum, passage_sum, query_grad, passage_grad):
    pairs_here = logits.shape[0]
    rest_rows = logits.shape[1] - QLEN
    entries = logits.shape[2]
    query_side = jnp.broadcast_to((query_grad / query_sum)[:, None, :], (pairs_here, QLEN, entries))
    passage_side = jnp.broadcast_to(
        (passage_grad / passage_sum)[:, None, :], (pairs_here, rest_rows, entries)
    )
    per_token = jnp.concatenate([query_side, passage_side], axis=1)
    slope = jax.nn.sigmoid(logits) / (1.0 + softened)
    return (boosted * slope * per_token).astype(jnp.bfloat16)


def per_device(hidden, head_weight, head_bias, lengths, positives):
    pairs_dev = lengths.shape[0]
    rows_pair = hidden.shape[0] // pairs_dev
    slice_width = head_bias.shape[0]
    vocab_devices = lax.axis_size("vocab")
    pairs_all = pairs_dev * lax.axis_size("dp")
    score_scale = 1.0 / (SCORE_TEMP * (slice_width * vocab_devices))
    weights = lax.all_gather(head_weight, "dp", axis=0, tiled=True)
    flat_logits = jnp.dot(hidden, weights, preferred_element_type=jnp.float32) + head_bias
    logits = flat_logits.reshape(pairs_dev, rows_pair, slice_width)
    token_mask = row_mask(lengths, rows_pair)
    softened, boosted = pool_terms(logits, token_mask)
    query_vec, passage_vec, query_sum, passage_sum = pooled_vectors(boosted, lengths)
    query_vec = query_vec.astype(jnp.bfloat16)
    passage_vec = passage_vec.astype(jnp.bfloat16)
    passages = lax.all_gather(passage_vec, "dp", axis=0, tiled=True)
    partial_value = lax.dot_general(
        query_vec, passages, (((1,), (1,)), ((), ())), preferred_element_type=jnp.float32
    )
    scores = score_scale * lax.psum(partial_value, "vocab")
    score_grad = score_grads(scores, positives, pairs_all)
    query_grad = score_scale * jnp.dot(
        score_grad, passages.astype(jnp.float32), precision=lax.Precision.HIGHEST
    )
    query_wide = query_vec.astype(jnp.float32)
    picked = score_grad
    passage_grad = score_scale * lax.psum_scatter(
        lax.dot_general(
            picked, query_wide, (((0,), (0,)), ((), ())), precision=lax.Precision.HIGHEST
        ),
        "dp",
        scatter_dimension=0,
        tiled=True,
    )
    logit_grad = logit_grads(
        logits, softened, boosted, query_sum, passage_sum, query_grad, passage_grad
    )
    logit_grad = logit_grad.reshape(pairs_dev * rows_pair, slice_width)
    picked = logit_grad
    summed = lax.psum_scatter(
        lax.dot_general(
            picked, weights, (((1,), (1,)), ((), ())), preferred_element_type=jnp.float32
        ),
        "vocab",
        scatter_dimension=0,
        tiled=True,
    )
    return summed.astype(jnp.bfloat16)


def solution(mesh):
    return jax.shard_map(
        per_device,
        mesh=mesh,
        in_specs=(P("dp", None), P("dp", "vocab"), P("vocab"), P("dp", None), P("dp")),
        out_specs=P(("dp", "vocab"), None),
        check_vma=False,
    )
```

profile of v0, /device:TPU:1, one launch (start us, length us, event | category | flops | bytes accessed | tf_op | source)
XLA Modules:
  0.0 666.8 jit_solution(6639236065506254835)
XLA Ops:
  6.5 0.7 all-gather.3.cloned.1.call-update
  7.5 1.0 slice_reduce_fusion.3
  8.8 1.0 convert_reduce_fusion.1
  9.9 77.3 %all-gather.3.cloned.1.call-done = bf16[4096,1024]{1,0:T(8,128)(2,1)} async-done(((bf16[128,1024]{1,0:T(8,128)(2,1)}), bf16[4096,1024]{1,0:T(8,128)(2,1)}) %all-gather.3.cloned.1.call-update) | async-done | bytes 8388624 | tf_op jit(solution)/shard_map/all_gather | solution.py:66
  87.2 5.4 convolution_add_fusion
  92.6 0.9 fusion.5
  93.7 41.5 %all-gather = bf16[32,2,1024]{2,1,0:T(2,128)(2,1)S(1)} all-gather(bf16[1,2,1024]{2,1,0:T(2,128)(2,1)S(1)} %fusion.8), channel_id=1, replica_groups=mesh['dp'=32,'vocab'=16] {'dp'}, dimensions={0}, use_global_device_ids=true | all-gather | bytes 135168 | tf_op jit(solution)/shard_map/all_gather | solution.py:74
  135.2 0.2 fusion.14
  135.5 46.5 %psum.7 = f32[2,64]{1,0:T(2,128)S(1)} all-reduce(f32[2,64]{1,0:T(2,128)S(1)} %fusion.14), channel_id=1, replica_groups=mesh['dp'=32,'vocab'=16] {'vocab'}, use_global_device_ids=true, to_apply=%region_2.3 | all-reduce | flops 128 | bytes 1024 | tf_op jit(solution)/shard_map/psum | solution.py:78
  182.0 0.2 fusion.10
  182.2 1.1 fusion.11
  183.4 1.3 dynamic-slice
  185.3 0.2 fusion.1
  185.5 275.8 %all-reduce.5.cloned.1.call-done = f32[64,1024]{1,0:T(8,128)} async-done(((f32[64,1024]{1,0:T(8,128)}), f32[64,1024]{1,0:T(8,128)}) %all-reduce.5.cloned.1.call-update) | async-done | bytes 262160
  461.3 0.8 fusion.7
  462.2 1.1 fusion.6
  463.4 7.9 %fusion.15 = f32[224,4096]{1,0:T(8,128)} fusion(bf16[224,1024]{1,0:T(8,128)(2,1)S(1)} %fusion.6, bf16[4096,1024]{1,0:T(8,128)(2,1)} %all-gather.3.cloned.1.call-done), kind=kOutput, calls=%fused_computation.38 | convolution fusion | flops 1879048192 | bytes 12517376 | tf_op jit(solution)/shard_map/dot_general | solution.py:99
  471.2 176.5 %fusion = f32[16,4096]{1,0:T(8,128)S(1)} fusion(f32[224,4096]{1,0:T(8,128)} %fusion.15), kind=kCustom, calls=%all-reduce-scatter | all-reduce-scatter fusion | flops 1048577 | bytes 3934208
  647.7 3.7 collective-permute-start
  651.4 1.7 collective-permute-start.1
  653.1 1.3 dynamic-slice.6
  655.0 3.6 collective-permute-done.1
  658.6 0.6 concatenate.7
  659.2 0.7 dynamic-slice_convert_fusion
  (30 shorter events, 1.2 us)
Async XLA Ops:
  6.5 80.7 %copy-start = (bf16[224,4096]{1,0:T(8,128)(2,1)S(1)}, bf16[224,4096]{1,0:T(8,128)(2,1)}, u32[]{:S(2)}) copy-start(bf16[224,4096]{1,0:T(8,128)(2,1)} %param.5) | copy-start | bytes 5505028
  6.5 80.7 %all-gather.3.cloned.1.call-start = ((), (), s32[]{:S(2)}) async-start(), calls=%async_computation | async-start | bytes 8650752 | tf_op jit(solution)/shard_map/all_gather | solution.py:66
  7.3 454.0 %all-reduce.5.cloned.1.call-start = ((), (), s32[]{:S(2)}) async-start(), calls=%async_computation.1 | async-start | bytes 524288
  9.9 172.4 %copy-start.1 = (s32[2]{0:T(128)S(1)}, s32[2]{0:T(128)}, u32[]{:S(2)}) copy-start(s32[2]{0:T(128)} %param.9) | copy-start | bytes 28
  647.7 10.9 %collective-permute-start = (bf16[16,4096]{1,0:T(8,128)(2,1)S(1)}, bf16[16,4096]{1,0:T(8,128)(2,1)S(1)}, u32[]{:S(2)}, u32[]{:S(2)}) collective-permute-start(bf16[16,4096]{1,0:T(8,128)(2,1)S(1)} %convert), channel_id=1, source_target_pairs={{0,1},{1,2},{2,3},{3,4},{4,5},{5,6},{6,7},{7,8},{8,9},{9,10},{10,1... | collective-permute-start | bytes 393224
  651.4 7.2 %collective-permute-start.1 = (bf16[14,4096]{1,0:T(8,128)(2,1)S(1)}, bf16[14,4096]{1,0:T(8,128)(2,1)S(1)}, u32[]{:S(2)}, u32[]{:S(2)}) collective-permute-start(bf16[14,4096]{1,0:T(8,128)(2,1)S(1)} %slice.20), channel_id=1, source_target_pairs={{0,2},{1,3},{2,4},{3,5},{4,6},{5,7},{6,8},{7,9},{8,10},{9,11},{10,... | collective-permute-start | bytes 344072
Sparse Core Ops, SparseCore 0:
  9.5 77.6 all-gather.2
  183.5 277.7 all-reduce.4
where the time goes:
time: 667 us
  waiting for transfers between devices  357 us (54%)
  blocking collectives  264 us (40%)
  matrix products  14.9 us (2%)
  between operations  14.9 us (2%)
    unnamed x5, waiting for transfers between devices  280 us
    unnamed x1, blocking collectives  176 us
    all_gather x1, waiting for transfers between devices, per_device(): weights = lax.all_gather(head_weight, 'dp', axis=0, tiled=True)  77.3 us
    psum x1, blocking collectives, per_device(): scores = score_scale * lax.psum(partial_value, 'vocab')  46.5 us
    all_gather x1, blocking collectives, per_device(): passages = lax.all_gather(passage_vec, 'dp', axis=0, tiled=True)  41.5 us
  transfers between devices with their start and end apart: 4, of which 3 were waited for; matrix products, arithmetic and copies ran while one was open for 1% of the time, Pallas kernels for 0%

commit v1 on v0

v1 whole, which is shorter than its diff:
```python
import jax
import jax.numpy as jnp
from jax import lax
from jax.experimental import pallas as pl
from jax.experimental.pallas import tpu as pltpu
from jax.sharding import PartitionSpec as P

QLEN = 32
PLEN = 80
ROWS_PAIR = QLEN + PLEN
ROWS = 2 * ROWS_PAIR
WIDTH = 4096
SLICE = 1024
SHARD = 128
HALF = 64
PAIRS = 64

POOL_TEMP = 0.25
SCORE_TEMP = 0.01
LOSS_SCALE = 65536.0
SCORE_SCALE = 1.0 / (SCORE_TEMP * 16384)

GROUP = 16
OWN = 14
CHUNK = 2 * GROUP
STREAMS = 8
COLS = WIDTH // STREAMS

BF = jnp.bfloat16
F32 = jnp.float32
MESH = pl.DeviceIdType.MESH

SEGMENTS = (
    (0, QLEN),
    (ROWS_PAIR, QLEN),
    (QLEN, PLEN),
    (ROWS_PAIR + QLEN, PLEN),
)


def kernel(
    hidden_ref, weight_ref, bias_ref, lengths_ref, positives_ref, out_ref,
    hid, wf, act, sums, vecs, packed, pooled, select, spread, both, part_scores, score_parts,
    grads, grads_t, targets, lgrad, part, chain_out, chain_in, kept, swap_out, swap_in,
    local_sem, w_send, w_recv, t_send, t_recv, v_send, v_recv, g_send, g_recv,
    s_send, s_recv, d_send, d_recv, c_send, c_recv, y_send, y_recv,
):
    dp = lax.axis_index("dp")
    vocab = lax.axis_index("vocab")
    x, y, core = dp // 8, (dp // 2) % 4, dp % 2
    z, hi = vocab // 2, vocab % 2
    xc = x * 2 + core

    def dp_of(xx, yy, cc):
        return (xx * 4 + yy) * 2 + cc

    load_w = pltpu.make_async_copy(weight_ref, wf.at[pl.ds(pl.multiple_of(dp * SHARD, SHARD), SHARD)], local_sem.at[0])
    load_h = pltpu.make_async_copy(hidden_ref, hid, local_sem.at[1])
    load_w.start()
    load_h.start()

    y_peers = [dp_of(x, (y + o) % 4, core) for o in range(1, 4)]
    xc_peers = [(xc + o) % 8 for o in range(1, 8)]
    xc_dp = [dp_of(p // 2, y, p % 2) for p in xc_peers]
    vocab_peers = [(vocab + o) % 16 for o in range(1, 16)]

    barrier = pltpu.get_barrier_semaphore()
    for p in y_peers + xc_dp:
        pl.semaphore_signal(barrier, inc=1, device_id={"dp": p, "vocab": vocab}, device_id_type=MESH)
    for p in vocab_peers:
        pl.semaphore_signal(barrier, inc=1, device_id={"dp": dp, "vocab": p}, device_id_type=MESH)

    row = lax.broadcasted_iota(jnp.int32, (128, 512), 0)
    col = lax.broadcasted_iota(jnp.int32, (128, 512), 1)
    pair = row % PAIRS
    first = (pair // 2) * 16 + pair % 2 + jnp.where(row < PAIRS, 2, 0)
    for i in range(4):
        select[i] = jnp.where(col == first + 4 * i, 1.0, 0.0).astype(BF)
    prow = lax.broadcasted_iota(jnp.int32, (256, 256), 0)
    pcol = lax.broadcasted_iota(jnp.int32, (256, 256), 1)
    wanted = (prow // GROUP) * OWN + prow % GROUP
    spread[...] = jnp.where((pcol == wanted) & (prow % GROUP < OWN), 1.0, 0.0).astype(BF)
    lgrad[pl.ds(ROWS, 32), :] = jnp.zeros((32, SLICE), BF)
    act[...] = jnp.broadcast_to(bias_ref[...], (ROWS, SLICE))

    trow = lax.broadcasted_iota(jnp.int32, (8, 128), 0)
    tcol = lax.broadcasted_iota(jnp.int32, (8, 128), 1)
    tile = jnp.zeros((8, 128), F32)
    for j in range(2):
        k = positives_ref[j]
        place = (k // 16) * 16 + ((k // 2) % 2) * 8 + ((k // 4) % 4) * 2 + k % 2
        tile = tile + jnp.where((trow == 2 * y + j) & (tcol == place), 1.0, 0.0)
    targets[y] = tile

    load_w.wait()
    pl.semaphore_wait(barrier, 25)

    sends = []

    def remote(src, dst, send_sem, recv_sem, to_dp, to_vocab):
        copy = pltpu.make_async_remote_copy(
            src_ref=src, dst_ref=dst, send_sem=send_sem, recv_sem=recv_sem,
            device_id={"dp": to_dp, "vocab": to_vocab}, device_id_type=MESH,
        )
        copy.start()
        return copy

    def unit(slot, h):
        return wf.at[pl.ds(pl.multiple_of(slot * SHARD + h * HALF, HALF), HALF)]

    def arrived(slot, h):
        pltpu.make_async_copy(unit(slot, h), unit(slot, h), w_recv.at[slot * 2 + h]).wait()

    count = [0]

    def send(slot, h, to, cond=None):
        n = count[0]
        count[0] += 1
        copy = pltpu.make_async_remote_copy(
            src_ref=unit(slot, h), dst_ref=unit(slot, h), send_sem=w_send.at[n], recv_sem=w_recv.at[slot * 2 + h],
            device_id={"dp": to, "vocab": vocab}, device_id_type=MESH,
        )
        if cond is None:
            copy.start()
        else:
            pl.when(cond)(copy.start)
        sends.append((cond, copy))

    right, left, far = (x + 1) % 4, (x + 3) % 4, (x + 2) % 4
    sibling = dp_of(x, y, 1 - core)

    def line_place(t):
        low = jnp.where(y < 2, y, 3 - y)
        place = jnp.where((low == 1) & (t < 2), 1 - t, t)
        return jnp.where(y < 2, place, 3 - place)

    def own_column(t):
        yy = line_place(t)
        slot = dp_of(x, yy, core)
        for h in range(2):
            if t == 0:
                send(slot, h, dp_of(x, jnp.minimum(y + 1, 3), core), y < 3)
                send(slot, h, dp_of(x, jnp.maximum(y - 1, 0), core), y > 0)
            else:
                arrived(slot, h)
                send(slot, h, dp_of(x, jnp.minimum(y + 1, 3), core), (yy < y) & (y < 3))
                send(slot, h, dp_of(x, jnp.maximum(y - 1, 0), core), (yy > y) & (y > 0))
            send(slot, h, dp_of(right, y, core))
            send(slot, h, dp_of(left, y, core))
            send(slot, h, sibling)

    def neighbours(t):
        yy = line_place(t)
        for h in range(2):
            slot = dp_of(left, yy, core)
            arrived(slot, h)
            if h == 0:
                send(slot, h, dp_of(right, y, core))
            send(slot, h, sibling)
            slot = dp_of(right, yy, core)
            arrived(slot, h)
            if h == 1:
                send(slot, h, dp_of(left, y, core))
            send(slot, h, sibling)

    def last(t):
        yy = line_place(t)
        slot = dp_of(far, yy, core)
        for h in range(2):
            arrived(slot, h)
            send(slot, h, sibling)

    def dots(t):
        yy = line_place(t)

        def step(i, carry):
            chip = ((x + i) % 4) * 4 + yy
            for h in range(2):
                arrived(chip * 2 + 1 - core, h)
            deep = pl.ds(pl.multiple_of(chip * 256, 256), 256)
            act[...] += jnp.dot(hid[:, deep], wf[deep, :], preferred_element_type=F32)
            return carry

        lax.fori_loop(0, 4, step, 0)

    own_column(0)
    t_copies = [
        remote(targets.at[y], targets.at[y], t_send.at[i], t_recv.at[y], p, vocab) for i, p in enumerate(y_peers)
    ]
    load_h.wait()
    own_column(1)
    neighbours(0)
    own_column(2)
    neighbours(1)
    last(0)
    dots(0)
    own_column(3)
    neighbours(2)
    last(1)
    dots(1)
    neighbours(3)
    last(2)
    dots(2)
    last(3)
    dots(3)

    def pool(b, carry):
        cols = pl.ds(pl.multiple_of(b * 128, 128), 128)
        for n, (start, size) in enumerate(SEGMENTS):
            length = lengths_ref[n % 2, n // 2]
            logits = act[pl.ds(start, size), cols]
            position = lax.broadcasted_iota(jnp.int32, (size, 128), 0)
            mask = jnp.where(position < length, 1.0, 0.0).astype(F32)
            small = jnp.exp(-jnp.abs(logits))
            above = 1.0 + jnp.maximum(logits, 0.0) + jnp.log1p(small)
            slope = jnp.where(logits >= 0.0, 1.0, small) / (1.0 + small)
            cubed = mask * (above * above * above)
            total = jnp.sum(cubed * above, axis=0, keepdims=True)
            act[pl.ds(start, size), cols] = cubed * slope
            sums[pl.ds(n, 1), cols] = total
            vecs[pl.ds(n, 1), cols] = POOL_TEMP * jnp.log(total / length.astype(F32))
        return carry

    lax.fori_loop(0, 8, pool, 0)
    for i in range(4):
        packed[pl.ds(4 * i, 4), :] = vecs[pl.ds(0, 4), pl.ds(256 * i, 256)]
    mine = xc * 4 + y
    pooled[mine] = packed[...].astype(BF)

    v_copies = [
        remote(pooled.at[mine], pooled.at[mine], v_send.at[i], v_recv.at[y], p, vocab) for i, p in enumerate(y_peers)
    ]
    for o in range(1, 4):
        yy = (y + o) % 4
        pltpu.make_async_copy(pooled.at[xc * 4 + yy], pooled.at[xc * 4 + yy], v_recv.at[yy]).wait()
    line = pl.ds(xc * 4, 4)
    g_copies = [
        remote(pooled.at[line], pooled.at[line], g_send.at[i], g_recv.at[xc], p, vocab) for i, p in enumerate(xc_dp)
    ]
    for p in xc_peers:
        block = pooled.at[pl.ds(p * 4, 4)]
        pltpu.make_async_copy(block, block, g_recv.at[p]).wait()

    flat = pooled[...].reshape(512, 256)
    for i in range(4):
        both[:, pl.ds(256 * i, 256)] = jnp.dot(select[i], flat, preferred_element_type=F32).astype(BF)
    nt = (((1,), (1,)), ((), ()))
    part_scores[...] = lax.dot_general(both[pl.ds(PAIRS, PAIRS), :], both[...], nt, preferred_element_type=F32)

    rows8 = pl.ds(pl.multiple_of(xc * 8, 8), 8)
    score_parts[vocab] = part_scores[rows8, :]
    s_copies = [
        remote(score_parts.at[vocab], score_parts.at[vocab], s_send.at[i], s_recv.at[vocab], dp, p)
        for i, p in enumerate(vocab_peers)
    ]
    for o in range(1, 4):
        yy = (y + o) % 4
        pltpu.make_async_copy(targets.at[yy], targets.at[yy], t_recv.at[yy]).wait()
    target = targets[0] + targets[1] + targets[2] + targets[3]
    for p in vocab_peers:
        pltpu.make_async_copy(score_parts.at[p], score_parts.at[p], s_recv.at[p]).wait()
    scores = SCORE_SCALE * jnp.sum(score_parts[...], axis=0)
    valid = tcol < PAIRS
    top = jnp.max(jnp.where(valid, scores, -jnp.inf), axis=1, keepdims=True)
    shifted = jnp.where(valid, jnp.exp(jnp.where(valid, scores - top, 0.0)), 0.0)
    soft = shifted / jnp.sum(shifted, axis=1, keepdims=True)
    grads[pl.ds(xc, 1)] = (LOSS_SCALE * (soft - target)).reshape(1, 8, 128)
    d_copies = [
        remote(grads.at[xc], grads.at[xc], d_send.at[i], d_recv.at[xc], p, vocab) for i, p in enumerate(xc_dp)
    ]
    for p in xc_peers:
        pltpu.make_async_copy(grads.at[p], grads.at[p], d_recv.at[p]).wait()
    whole = jnp.concatenate([grads[...].reshape(PAIRS, 128), jnp.zeros((PAIRS, 128), F32)], axis=0)
    grads_t[...] = whole.T

    def exact_dot(lhs, rhs):
        a = lhs.astype(BF)
        rest = lhs - a.astype(F32)
        b = rest.astype(BF)
        c = (rest - b.astype(F32)).astype(BF)
        out = jnp.dot(c, rhs, preferred_element_type=F32)
        out = out + jnp.dot(b, rhs, preferred_element_type=F32)
        return out + jnp.dot(a, rhs, preferred_element_type=F32)

    q_grad = exact_dot(grads[pl.ds(xc, 1)].reshape(8, 128)[:, :PAIRS], both[pl.ds(0, PAIRS), :])
    p_grad = exact_dot(grads_t[rows8, :][:, :PAIRS], both[pl.ds(PAIRS, PAIRS), :])
    srow = lax.broadcasted_iota(jnp.int32, (8, SLICE), 0)
    for n, (start, size) in enumerate(SEGMENTS):
        grad = q_grad if n < 2 else p_grad
        one = jnp.sum(jnp.where(srow == 2 * y + n % 2, grad, 0.0), axis=0, keepdims=True)
        vecs[pl.ds(n, 1), :] = (SCORE_SCALE * one) / sums[pl.ds(n, 1), :]

    def finish(b, carry):
        cols = pl.ds(pl.multiple_of(b * 128, 128), 128)
        for n, (start, size) in enumerate(SEGMENTS):
            lgrad[pl.ds(start, size), cols] = (act[pl.ds(start, size), cols] * vecs[pl.ds(n, 1), cols]).astype(BF)
        return carry

    lax.fori_loop(0, 8, finish, 0)
    lgrad[...] = jnp.dot(spread[...], lgrad[...], preferred_element_type=F32).astype(BF)

    up, down = ((z + 1) % 8) * 2 + hi, ((z + 7) % 8) * 2 + hi
    across = z * 2 + 1 - hi
    c_copies = []

    def place(k):
        return pl.ds(pl.multiple_of(((z + k + 8) % 8) * CHUNK, CHUNK), CHUNK)

    def hop(c, i, value, to):
        chain_out[c, i] = value.astype(BF)
        c_copies.append(remote(chain_out.at[c, i], chain_in.at[c, i], c_send.at[c, i], c_recv.at[c, i], dp, to))

    def landed(c, i):
        pltpu.make_async_copy(chain_in.at[c, i], chain_in.at[c, i], c_recv.at[c, i]).wait()
        return chain_in[c, i].astype(F32)

    def advance(c, s):
        a = 4 if c % 2 == 0 else 3
        b = 7 - a
        cols = pl.ds(c * COLS, COLS)
        if s == 0:
            part[:, cols] = lax.dot_general(lgrad[...], wf[cols, :], nt, preferred_element_type=F32)
            hop(c, 0, part[place(a), cols], up)
            hop(c, a, part[place(-b), cols], down)
        elif s < 4:
            if s < a:
                hop(c, s, landed(c, s - 1) + part[place(a - s), cols], up)
            if s < b:
                hop(c, a + s, landed(c, a + s - 1) + part[place(s - b), cols], down)
        elif s == 4:
            total = part[place(0), cols] + landed(c, a - 1) + landed(c, 6)
            kept[c] = total
            swap_out[c] = kept[c, pl.ds(pl.multiple_of((1 - hi) * GROUP, GROUP), GROUP), :].astype(BF)
            c_copies.append(remote(swap_out.at[c], swap_in.at[c], y_send.at[c], y_recv.at[c], dp, across))
        else:
            pltpu.make_async_copy(swap_in.at[c], swap_in.at[c], y_recv.at[c]).wait()
            total = kept[c, pl.ds(pl.multiple_of(hi * GROUP, GROUP), GROUP), :] + swap_in[c].astype(F32)
            out_ref[:, cols] = total[:OWN].astype(BF)

    for t in range(STREAMS + 5):
        for c in range(STREAMS):
            if 0 <= t - c <= 5:
                advance(c, t - c)

    for cond, copy in sends:
        if cond is None:
            copy.wait_send()
        else:
            pl.when(cond)(copy.wait_send)
    for copy in t_copies + v_copies + g_copies + s_copies + d_copies + c_copies:
        copy.wait_send()


def per_device(hidden, head_weight, head_bias, lengths, positives):
    vmem, smem = pltpu.VMEM, pltpu.SMEM
    dma = pltpu.SemaphoreType.DMA
    return pl.pallas_call(
        kernel,
        out_shape=jax.ShapeDtypeStruct((OWN, WIDTH), BF),
        in_specs=[
            pl.BlockSpec(memory_space=pl.ANY),
            pl.BlockSpec(memory_space=pl.ANY),
            pl.BlockSpec(memory_space=vmem),
            pl.BlockSpec(memory_space=smem),
            pl.BlockSpec(memory_space=smem),
        ],
        out_specs=pl.BlockSpec(memory_space=vmem),
        scratch_shapes=[
            vmem((ROWS, WIDTH), BF),
            vmem((WIDTH, SLICE), BF),
            vmem((ROWS, SLICE), F32),
            vmem((8, SLICE), F32),
            vmem((8, SLICE), F32),
            vmem((16, 256), F32),
            vmem((32, 16, 256), BF),
            vmem((4, 128, 512), BF),
            vmem((256, 256), BF),
            vmem((128, SLICE), BF),
            vmem((PAIRS, 128), F32),
            vmem((16, 8, 128), F32),
            vmem((8, 8, 128), F32),
            vmem((128, 128), F32),
            vmem((4, 8, 128), F32),
            vmem((256, SLICE), BF),
            vmem((256, WIDTH), F32),
            vmem((STREAMS, 7, CHUNK, COLS), BF),
            vmem((STREAMS, 7, CHUNK, COLS), BF),
            vmem((STREAMS, CHUNK, COLS), F32),
            vmem((STREAMS, GROUP, COLS), BF),
            vmem((STREAMS, GROUP, COLS), BF),
            dma((2,)),
            dma((96,)), dma((64,)),
            dma((3,)), dma((4,)),
            dma((3,)), dma((4,)),
            dma((7,)), dma((8,)),
            dma((15,)), dma((16,)),
            dma((7,)), dma((8,)),
            dma((STREAMS, 7)), dma((STREAMS, 7)),
            dma((STREAMS,)), dma((STREAMS,)),
        ],
        compiler_params=pltpu.CompilerParams(
            collective_id=0, has_side_effects=True, vmem_limit_bytes=48 * 1024 * 1024
        ),
        cost_estimate=pl.CostEstimate(flops=4 * ROWS * WIDTH * SLICE, bytes_accessed=4 * 1024 * 1024, transcendentals=3 * ROWS * SLICE),
    )(hidden, head_weight, head_bias.reshape(1, SLICE), lengths, positives)


def solution(mesh):
    return jax.shard_map(
        per_device,
        mesh=mesh,
        in_specs=(P("dp", None), P("dp", "vocab"), P("vocab"), P("dp", None), P("dp")),
        out_specs=P(("dp", "vocab"), None),
        check_vma=False,
    )
```

time: 667 us -> 137 us (0.21)
  the two profiles are of different devices: /device:TPU:1 before, /device:TPU:56 now
where the time goes in v1:
time: 137 us
  Pallas kernels  132 us (96%)
  local copies, waits for them, and re-layouts  5.13 us (4%)
    pallas_call x1, Pallas kernels, per_device(): pl.pallas_call(kernel, out_shape=jax.ShapeDtypeStruct((OWN, WIDTH), BF),...  132 us
    unnamed x11, local copies, waits for them, and re-layouts  5.13 us

profile of v1, /device:TPU:56, one launch (start us, length us, event | category | flops | bytes accessed | tf_op | source)
XLA Modules:
  0.0 136.7 jit_solution(15249919144493144797)
XLA Ops:
  0.0 0.0 copy-start
  0.0 1.5 %copy-done = bf16[224,4096]{1,0:T(8,128)(2,1)S(1)} copy-done((bf16[224,4096]{1,0:T(8,128)(2,1)S(1)}, bf16[224,4096]{1,0:T(8,128)(2,1)}, u32[]{:S(2)}) %copy-start) | copy-done | bytes 1835032
  1.5 0.0 copy-start.1
  1.5 0.9 copy-done.1
  2.5 0.0 copy-start.2
  2.5 0.7 copy-done.2
  3.1 0.0 copy-start.3
  3.1 0.7 copy-done.3
  3.8 0.0 copy-start.4
  3.8 0.7 copy-done.4
  4.5 131.6 %shard_map.55 = bf16[14,4096]{1,0:T(8,128)(2,1)S(1)} custom-call(bf16[224,4096]{1,0:T(8,128)(2,1)S(1)} %copy-done, bf16[128,1024]{1,0:T(8,128)(2,1)S(1)} %copy-done.1, f32[1,1024]{1,0:T(1,128)S(1)} %bitcast.1, s32[2,2]{1,0:T(2,128)S(1)} %copy-done.3, s32[2]{0:T(128)S(1)} %copy-done.4), custom_call_target="tpu_custom_call" | custom-call | flops 3758096384 | bytes 4194304 | tf_op jit(solution)/shard_map/pallas_call | solution.py:357
  136.0 0.7 copy.7
Async XLA Ops:
  0.0 1.5 %copy-start = (bf16[224,4096]{1,0:T(8,128)(2,1)S(1)}, bf16[224,4096]{1,0:T(8,128)(2,1)}, u32[]{:S(2)}) copy-start(bf16[224,4096]{1,0:T(8,128)(2,1)} %hidden_ref.1) | copy-start | bytes 5505028
  1.5 0.9 copy-start.1
  2.5 0.7 copy-start.2
  3.1 0.7 copy-start.3
  3.8 0.7 copy-start.4

commit v2 on v1

v2 whole, which is shorter than its diff:
```python
import jax
import jax.numpy as jnp
from jax import lax
from jax.experimental import pallas as pl
from jax.experimental.pallas import tpu as pltpu
from jax.sharding import PartitionSpec as P

QLEN = 32
PLEN = 80
ROWS_PAIR = QLEN + PLEN
ROWS = 2 * ROWS_PAIR
WIDTH = 4096
SLICE = 1024
SHARD = 128
PAIRS = 64

POOL_TEMP = 0.25
SCORE_TEMP = 0.01
LOSS_SCALE = 65536.0
SCORE_SCALE = 1.0 / (SCORE_TEMP * 16384)

GROUP = 16
OWN = 14
CHUNK = 2 * GROUP
STREAMS = 8
COLS = WIDTH // STREAMS
EARLY = 1
LAG = 8

BF = jnp.bfloat16
F32 = jnp.float32
MESH = pl.DeviceIdType.MESH

SEGMENTS = (
    (0, QLEN),
    (ROWS_PAIR, QLEN),
    (QLEN, PLEN),
    (ROWS_PAIR + QLEN, PLEN),
)


def kernel(
    hidden_ref, weight_ref, bias_hbm, lengths_hbm, positives_hbm, out_ref,
    bias_ref, lengths_ref, positives_ref, hid, wf, act, sums, vecs, packed, pooled, select, spread, both, part_scores, score_parts,
    grads, grads_t, targets, lgrad, part, chain_out, chain_in, kept, swap_out, swap_in,
    wide_out, wide_in, near_out, near_in, summed,
    local_sem, w_send, w_recv, t_send, t_recv, v_send, v_recv, g_send, g_recv,
    s_send, s_recv, d_send, d_recv, c_send, c_recv, y_send, y_recv,
):
    dp = lax.axis_index("dp")
    vocab = lax.axis_index("vocab")
    x, y, core = dp // 8, (dp // 2) % 4, dp % 2
    z, hi = vocab // 2, vocab % 2
    xc = x * 2 + core

    def dp_of(xx, yy, cc):
        return (xx * 4 + yy) * 2 + cc

    load_w = pltpu.make_async_copy(weight_ref, wf.at[pl.ds(pl.multiple_of(dp * SHARD, SHARD), SHARD)], local_sem.at[0])
    load_h = pltpu.make_async_copy(hidden_ref, hid, local_sem.at[1])
    loads = [
        load_w,
        load_h,
        pltpu.make_async_copy(bias_hbm, bias_ref, local_sem.at[2]),
        pltpu.make_async_copy(lengths_hbm, lengths_ref, local_sem.at[3]),
        pltpu.make_async_copy(positives_hbm, positives_ref, local_sem.at[4]),
    ]
    for load in loads:
        load.start()

    y_peers = [dp_of(x, (y + o) % 4, core) for o in range(1, 4)]
    xc_peers = [(xc + o) % 8 for o in range(1, 8)]
    xc_dp = [dp_of(p // 2, y, p % 2) for p in xc_peers]
    vocab_peers = [(vocab + o) % 16 for o in range(1, 16)]

    barrier = pltpu.get_barrier_semaphore()
    for p in y_peers + xc_dp:
        pl.semaphore_signal(barrier, inc=1, device_id={"dp": p, "vocab": vocab}, device_id_type=MESH)
    for p in vocab_peers:
        pl.semaphore_signal(barrier, inc=1, device_id={"dp": dp, "vocab": p}, device_id_type=MESH)

    load_w.wait()
    pl.semaphore_wait(barrier, 25)

    sends = []
    copies = []

    def remote(src, dst, send_sem, recv_sem, to_dp, to_vocab):
        copy = pltpu.make_async_remote_copy(
            src_ref=src, dst_ref=dst, send_sem=send_sem, recv_sem=recv_sem,
            device_id={"dp": to_dp, "vocab": to_vocab}, device_id_type=MESH,
        )
        copy.start()
        copies.append(copy)

    UNITS = ((0, 64), (64, 48), (112, 16))
    FIRST, REST = (0, 1), 2

    def unit(slot, u):
        start, size = UNITS[u]
        return wf.at[pl.ds(pl.multiple_of(slot * SHARD + start, 16), size)]

    def w_sem(slot, u):
        return w_recv.at[slot * 3 + u]

    def arrived(slot, u):
        pltpu.make_async_copy(unit(slot, u), unit(slot, u), w_sem(slot, u)).wait()

    count = [0]

    def send(slot, u, to, cond=None):
        n = count[0]
        count[0] += 1
        copy = pltpu.make_async_remote_copy(
            src_ref=unit(slot, u), dst_ref=unit(slot, u), send_sem=w_send.at[n], recv_sem=w_sem(slot, u),
            device_id={"dp": to, "vocab": vocab}, device_id_type=MESH,
        )
        if cond is None:
            copy.start()
        else:
            pl.when(cond)(copy.start)
        sends.append((cond, copy))

    right, left, far = (x + 1) % 4, (x + 3) % 4, (x + 2) % 4
    to_right, to_left = dp_of(right, y, core), dp_of(left, y, core)
    above, below = dp_of(x, jnp.minimum(y + 1, 3), core), dp_of(x, jnp.maximum(y - 1, 0), core)
    sibling = dp_of(x, y, 1 - core)

    def line_place(t):
        low = jnp.where(y < 2, y, 3 - y)
        place = jnp.where((low == 1) & (t < 2), 1 - t, t)
        return jnp.where(y < 2, place, 3 - place)

    def onward(slot, u, yy):
        rising = yy < y
        send(slot, u, jnp.where(rising, above, below), (rising & (y < 3)) | ((yy > y) & (y > 0)))

    def both_ways(slot, u):
        send(slot, u, above, y < 3)
        send(slot, u, below, y > 0)

    def column(t):
        yy = line_place(t)
        slot = dp_of(x, yy, core)
        for u in FIRST:
            if t == 0:
                both_ways(slot, u)
            else:
                arrived(slot, u)
                onward(slot, u, yy)
            send(slot, u, to_right)
            send(slot, u, to_left)
            send(slot, u, sibling)

    def relay(u, yy):
        rightward = (yy + u) % 2 == 0
        slot = dp_of(jnp.where(rightward, left, right), yy, core)
        arrived(slot, u)
        send(slot, u, jnp.where(rightward, to_right, to_left))
        send(slot, u, sibling)
        slot = dp_of(jnp.where(rightward, right, left), yy, core)
        arrived(slot, u)
        send(slot, u, sibling)

    def neighbours(t):
        for u in FIRST:
            relay(u, line_place(t))

    def last(t):
        slot = dp_of(far, line_place(t), core)
        for u in FIRST:
            arrived(slot, u)
            send(slot, u, sibling)

    def rest_own():
        send(dp, REST, to_right)
        send(dp, REST, to_left)
        send(dp, REST, sibling)

    def rest_neighbours():
        relay(REST, y)

    def rest_out():
        for source in (x, left, right):
            both_ways(dp_of(source, y, core), REST)

    def rest_last():
        slot = dp_of(far, y, core)
        arrived(slot, REST)
        both_ways(slot, REST)
        send(slot, REST, sibling)

    def rest_line(t):
        yy = line_place(t)
        for source in (x, left, right, far):
            slot = dp_of(source, yy, core)
            arrived(slot, REST)
            onward(slot, REST, yy)
            send(slot, REST, sibling)

    def dots(t):
        yy = line_place(t)

        def step(i, carry):
            chip = ((x + 3 + i) % 4) * 4 + yy
            for u in FIRST + (REST,):
                arrived(chip * 2 + 1 - core, u)
            deep = pl.ds(pl.multiple_of(chip * 256, 256), 256)
            act[...] += jnp.dot(hid[:, deep], wf[deep, :], preferred_element_type=F32)
            return carry

        lax.fori_loop(0, 4, step, 0)

    column(0)
    rest_own()

    for load in loads[1:]:
        load.wait()

    row = lax.broadcasted_iota(jnp.int32, (128, 512), 0)
    col = lax.broadcasted_iota(jnp.int32, (128, 512), 1)
    pair = row % PAIRS
    first = (pair // 2) * 16 + pair % 2 + jnp.where(row < PAIRS, 2, 0)
    for i in range(4):
        select[i] = jnp.where(col == first + 4 * i, 1.0, 0.0).astype(BF)
    prow = lax.broadcasted_iota(jnp.int32, (256, 256), 0)
    pcol = lax.broadcasted_iota(jnp.int32, (256, 256), 1)
    wanted = (prow // GROUP) * OWN + prow % GROUP
    spread[...] = jnp.where((pcol == wanted) & (prow % GROUP < OWN), 1.0, 0.0).astype(BF)
    lgrad[pl.ds(ROWS, 32), :] = jnp.zeros((32, SLICE), BF)
    act[...] = jnp.broadcast_to(bias_ref[...], (ROWS, SLICE))

    trow = lax.broadcasted_iota(jnp.int32, (8, 128), 0)
    tcol = lax.broadcasted_iota(jnp.int32, (8, 128), 1)
    tile = jnp.zeros((8, 128), F32)
    for j in range(2):
        k = positives_ref[j]
        place = (k // 16) * 16 + ((k // 2) % 2) * 8 + ((k // 4) % 4) * 2 + k % 2
        tile = tile + jnp.where((trow == 2 * y + j) & (tcol == place), 1.0, 0.0)
    targets[y] = tile

    for i, p in enumerate(y_peers):
        remote(targets.at[y], targets.at[y], t_send.at[i], t_recv.at[y], p, vocab)
    column(1)
    neighbours(0)
    column(2)
    rest_neighbours()
    neighbours(1)
    column(3)
    rest_out()
    last(0)
    rest_last()
    neighbours(2)
    rest_line(1)
    last(1)
    neighbours(3)
    rest_line(2)
    last(2)
    rest_line(3)
    last(3)
    for t in range(4):
        dots(t)
    for o in range(1, 4):
        yy = (y + o) % 4
        pltpu.make_async_copy(targets.at[yy], targets.at[yy], t_recv.at[yy]).wait()

    def pool(b, carry):
        cols = pl.ds(pl.multiple_of(b * 128, 128), 128)
        for n, (start, size) in enumerate(SEGMENTS):
            length = lengths_ref[n % 2, n // 2]
            logits = act[pl.ds(start, size), cols]
            position = lax.broadcasted_iota(jnp.int32, (size, 128), 0)
            mask = jnp.where(position < length, 1.0, 0.0).astype(F32)
            small = jnp.exp(-jnp.abs(logits))
            above = 1.0 + jnp.maximum(logits, 0.0) + jnp.log1p(small)
            slope = jnp.where(logits >= 0.0, 1.0, small) / (1.0 + small)
            cubed = mask * (above * above * above)
            total = jnp.sum(cubed * above, axis=0, keepdims=True)
            act[pl.ds(start, size), cols] = cubed * slope
            sums[pl.ds(n, 1), cols] = total
            vecs[pl.ds(n, 1), cols] = POOL_TEMP * jnp.log(total / length.astype(F32))
        return carry

    lax.fori_loop(0, 8, pool, 0)
    for i in range(4):
        packed[pl.ds(4 * i, 4), :] = vecs[pl.ds(0, 4), pl.ds(256 * i, 256)]
    mine = xc * 4 + y
    pooled[mine] = packed[...].astype(BF)

    for i, p in enumerate(y_peers):
        remote(pooled.at[mine], pooled.at[mine], v_send.at[i], v_recv.at[y], p, vocab)
    for o in range(1, 4):
        yy = (y + o) % 4
        pltpu.make_async_copy(pooled.at[xc * 4 + yy], pooled.at[xc * 4 + yy], v_recv.at[yy]).wait()
    line = pl.ds(xc * 4, 4)
    for i, p in enumerate(xc_dp):
        remote(pooled.at[line], pooled.at[line], g_send.at[i], g_recv.at[xc], p, vocab)
    for p in xc_peers:
        block = pooled.at[pl.ds(p * 4, 4)]
        pltpu.make_async_copy(block, block, g_recv.at[p]).wait()

    flat = pooled[...].reshape(512, 256)
    for i in range(4):
        both[:, pl.ds(256 * i, 256)] = jnp.dot(select[i], flat, preferred_element_type=F32).astype(BF)
    nt = (((1,), (1,)), ((), ()))
    part_scores[...] = lax.dot_general(both[pl.ds(PAIRS, PAIRS), :], both[...], nt, preferred_element_type=F32)

    rows8 = pl.ds(pl.multiple_of(xc * 8, 8), 8)
    score_parts[vocab] = part_scores[rows8, :]
    for i, p in enumerate(vocab_peers):
        remote(score_parts.at[vocab], score_parts.at[vocab], s_send.at[i], s_recv.at[vocab], dp, p)
    target = targets[0] + targets[1] + targets[2] + targets[3]
    for p in vocab_peers:
        pltpu.make_async_copy(score_parts.at[p], score_parts.at[p], s_recv.at[p]).wait()
    scores = SCORE_SCALE * jnp.sum(score_parts[...], axis=0)
    valid = tcol < PAIRS
    top = jnp.max(jnp.where(valid, scores, -jnp.inf), axis=1, keepdims=True)
    shifted = jnp.where(valid, jnp.exp(jnp.where(valid, scores - top, 0.0)), 0.0)
    soft = shifted / jnp.sum(shifted, axis=1, keepdims=True)
    grads[pl.ds(xc, 1)] = (LOSS_SCALE * (soft - target)).reshape(1, 8, 128)
    for i, p in enumerate(xc_dp):
        remote(grads.at[xc], grads.at[xc], d_send.at[i], d_recv.at[xc], p, vocab)
    for p in xc_peers:
        pltpu.make_async_copy(grads.at[p], grads.at[p], d_recv.at[p]).wait()
    whole = jnp.concatenate([grads[...].reshape(PAIRS, 128), jnp.zeros((PAIRS, 128), F32)], axis=0)
    grads_t[...] = whole.T

    def exact_dot(lhs, rhs):
        a = lhs.astype(BF)
        rest = lhs - a.astype(F32)
        b = rest.astype(BF)
        c = (rest - b.astype(F32)).astype(BF)
        out = jnp.dot(c, rhs, preferred_element_type=F32)
        out = out + jnp.dot(b, rhs, preferred_element_type=F32)
        return out + jnp.dot(a, rhs, preferred_element_type=F32)

    q_grad = exact_dot(grads[pl.ds(xc, 1)].reshape(8, 128)[:, :PAIRS], both[pl.ds(0, PAIRS), :])
    p_grad = exact_dot(grads_t[rows8, :][:, :PAIRS], both[pl.ds(PAIRS, PAIRS), :])
    srow = lax.broadcasted_iota(jnp.int32, (8, SLICE), 0)
    for n, (start, size) in enumerate(SEGMENTS):
        grad = q_grad if n < 2 else p_grad
        one = jnp.sum(jnp.where(srow == 2 * y + n % 2, grad, 0.0), axis=0, keepdims=True)
        vecs[pl.ds(n, 1), :] = (SCORE_SCALE * one) / sums[pl.ds(n, 1), :]

    def finish(b, carry):
        cols = pl.ds(pl.multiple_of(b * 128, 128), 128)
        for n, (start, size) in enumerate(SEGMENTS):
            lgrad[pl.ds(start, size), cols] = (act[pl.ds(start, size), cols] * vecs[pl.ds(n, 1), cols]).astype(BF)
        return carry

    lax.fori_loop(0, 8, finish, 0)
    lgrad[...] = jnp.dot(spread[...], lgrad[...], preferred_element_type=F32).astype(BF)

    up, down = ((z + 1) % 8) * 2 + hi, ((z + 7) % 8) * 2 + hi
    across = z * 2 + 1 - hi

    def cols_of(c):
        return pl.ds(c * COLS, COLS)

    def own_part(c, k):
        place = (z + k + 8) % 8
        if c < EARLY:
            return summed[c, place]
        return part[pl.ds(pl.multiple_of(place * CHUNK, CHUNK), CHUNK), cols_of(c)]

    def hop(c, i, value, to):
        if c < EARLY:
            out_slot, in_slot = near_out.at[c, i], near_in.at[c, i]
        else:
            out_slot, in_slot = chain_out.at[c - EARLY, i], chain_in.at[c - EARLY, i]
        out_slot[...] = value.astype(BF)
        remote(out_slot, in_slot, c_send.at[c, i], c_recv.at[c, i], dp, to)

    def landed(c, i):
        in_slot = near_in.at[c, i] if c < EARLY else chain_in.at[c - EARLY, i]
        pltpu.make_async_copy(in_slot, in_slot, c_recv.at[c, i]).wait()
        return in_slot[...].astype(F32)

    def chain(c, s):
        a = 4 if c % 2 == 0 else 3
        b = 7 - a
        if s == 0:
            hop(c, 0, own_part(c, a), up)
            hop(c, a, own_part(c, -b), down)
        elif s < 4:
            if s < a:
                hop(c, s, landed(c, s - 1) + own_part(c, a - s), up)
            if s < b:
                hop(c, a + s, landed(c, a + s - 1) + own_part(c, s - b), down)
        else:
            return own_part(c, 0) + landed(c, a - 1) + landed(c, 6)

    def product(c):
        part[:, cols_of(c)] = lax.dot_general(lgrad[...], wf[cols_of(c), :], nt, preferred_element_type=F32)

    def group(c, place, h):
        return part[pl.ds(pl.multiple_of(place * CHUNK + h * GROUP, GROUP), GROUP), cols_of(c)]

    def early(c, s):
        if s == 0:
            product(c)
            for place in range(8):
                wide_out[c, place] = group(c, place, 1 - hi).astype(BF)
            remote(wide_out.at[c], wide_in.at[c], y_send.at[c], y_recv.at[c], dp, across)
        elif s == 1:
            pltpu.make_async_copy(wide_in.at[c], wide_in.at[c], y_recv.at[c]).wait()
            for place in range(8):
                summed[c, place] = group(c, place, hi) + wide_in[c, place].astype(F32)
            chain(c, 0)
        elif s < 5:
            chain(c, s - 1)
        else:
            out_ref[:, cols_of(c)] = chain(c, 4)[:OWN].astype(BF)

    def late(c, s):
        if s == 0:
            product(c)
        if s < 4:
            chain(c, s)
        elif s == 4:
            kept[c] = chain(c, 4)
            swap_out[c] = kept[c, pl.ds(pl.multiple_of((1 - hi) * GROUP, GROUP), GROUP), :].astype(BF)
            remote(swap_out.at[c], swap_in.at[c], y_send.at[c], y_recv.at[c], dp, across)
        else:
            pltpu.make_async_copy(swap_in.at[c], swap_in.at[c], y_recv.at[c]).wait()
            total = kept[c, pl.ds(pl.multiple_of(hi * GROUP, GROUP), GROUP), :] + swap_in[c].astype(F32)
            out_ref[:, cols_of(c)] = total[:OWN].astype(BF)

    def when(c, s):
        if c < EARLY:
            return (STREAMS * s + c + (LAG if s else 0), c)
        return (STREAMS * s + c, c)

    for c, s in sorted(((c, s) for c in range(STREAMS) for s in range(6)), key=lambda e: when(*e)):
        (early if c < EARLY else late)(c, s)

    for cond, copy in sends:
        if cond is None:
            copy.wait_send()
        else:
            pl.when(cond)(copy.wait_send)
    for copy in copies:
        copy.wait_send()


def per_device(hidden, head_weight, head_bias, lengths, positives):
    vmem, smem = pltpu.VMEM, pltpu.SMEM
    dma = pltpu.SemaphoreType.DMA
    return pl.pallas_call(
        kernel,
        out_shape=jax.ShapeDtypeStruct((OWN, WIDTH), BF),
        in_specs=[
            pl.BlockSpec(memory_space=pl.ANY),
            pl.BlockSpec(memory_space=pl.ANY),
            pl.BlockSpec(memory_space=pl.ANY),
            pl.BlockSpec(memory_space=pl.ANY),
            pl.BlockSpec(memory_space=pl.ANY),
        ],
        out_specs=pl.BlockSpec(memory_space=vmem),
        scratch_shapes=[
            vmem((1, SLICE), F32),
            smem((2, 2), jnp.int32),
            smem((2,), jnp.int32),
            vmem((ROWS, WIDTH), BF),
            vmem((WIDTH, SLICE), BF),
            vmem((ROWS, SLICE), F32),
            vmem((8, SLICE), F32),
            vmem((8, SLICE), F32),
            vmem((16, 256), F32),
            vmem((32, 16, 256), BF),
            vmem((4, 128, 512), BF),
            vmem((256, 256), BF),
            vmem((128, SLICE), BF),
            vmem((PAIRS, 128), F32),
            vmem((16, 8, 128), F32),
            vmem((8, 8, 128), F32),
            vmem((128, 128), F32),
            vmem((4, 8, 128), F32),
            vmem((256, SLICE), BF),
            vmem((256, WIDTH), F32),
            vmem((STREAMS - EARLY, 7, CHUNK, COLS), BF),
            vmem((STREAMS - EARLY, 7, CHUNK, COLS), BF),
            vmem((STREAMS, CHUNK, COLS), F32),
            vmem((STREAMS, GROUP, COLS), BF),
            vmem((STREAMS, GROUP, COLS), BF),
            vmem((EARLY, 8, GROUP, COLS), BF),
            vmem((EARLY, 8, GROUP, COLS), BF),
            vmem((EARLY, 7, GROUP, COLS), BF),
            vmem((EARLY, 7, GROUP, COLS), BF),
            vmem((EARLY, 8, GROUP, COLS), F32),
            dma((5,)),
            dma((128,)), dma((96,)),
            dma((3,)), dma((4,)),
            dma((3,)), dma((4,)),
            dma((7,)), dma((8,)),
            dma((15,)), dma((16,)),
            dma((7,)), dma((8,)),
            dma((STREAMS, 7)), dma((STREAMS, 7)),
            dma((STREAMS,)), dma((STREAMS,)),
        ],
        compiler_params=pltpu.CompilerParams(
            collective_id=0, has_side_effects=True, vmem_limit_bytes=63 * 1024 * 1024
        ),
        cost_estimate=pl.CostEstimate(flops=4 * ROWS * WIDTH * SLICE, bytes_accessed=4 * 1024 * 1024, transcendentals=3 * ROWS * SLICE),
    )(hidden, head_weight, head_bias.reshape(1, SLICE), lengths, positives)


def solution(mesh):
    return jax.shard_map(
        per_device,
        mesh=mesh,
        in_specs=(P("dp", None), P("dp", "vocab"), P("vocab"), P("dp", None), P("dp")),
        out_specs=P(("dp", "vocab"), None),
        check_vma=False,
    )
```

time: 137 us -> 112 us (0.82)
  the two profiles are of different devices: /device:TPU:56 before, /device:TPU:1 now
where the time goes in v2:
time: 112 us
  Pallas kernels  111 us (99%)
  local copies, waits for them, and re-layouts  1.57 us (1%)
    pallas_call x1, Pallas kernels, per_device(): pl.pallas_call(kernel, out_shape=jax.ShapeDtypeStruct((OWN, WIDTH), BF),...  111 us

profile of v2, /device:TPU:1, one launch (start us, length us, event | category | flops | bytes accessed | tf_op | source)
XLA Modules:
  0.0 112.3 jit_solution(4650988532577400397)
XLA Ops:
  0.0 110.8 %shard_map.55 = bf16[14,4096]{1,0:T(8,128)(2,1)} custom-call(bf16[224,4096]{1,0:T(8,128)(2,1)} %hidden_ref.1, bf16[128,1024]{1,0:T(8,128)(2,1)} %weight_ref.1, f32[1,1024]{1,0:T(1,128)} %bitcast.1, s32[2,2]{1,0:T(2,128)} %lengths_hbm.1, s32[2]{0:T(128)} %positives_hbm.1), custom_call_target="tpu_custom_call" | custom-call | flops 3758096384 | bytes 4194304 | tf_op jit(solution)/shard_map/pallas_call | solution.py:449
  110.8 1.6 %copy.7 = bf16[14,4096]{1,0:T(8,128)(2,1)} copy(bf16[14,4096]{1,0:T(8,128)(2,1)} %shard_map.55) | data formatting | bytes 229376

commit v3 on v2

--- a/solution.py
+++ b/solution.py
@@ -41,17 +41,17 @@
 
 def kernel(
     hidden_ref, weight_ref, bias_hbm, lengths_hbm, positives_hbm, out_ref,
-    bias_ref, lengths_ref, positives_ref, hid, wf, act, sums, vecs, packed, pooled, select, spread, both, part_scores, score_parts,
-    grads, grads_t, targets, lgrad, part, chain_out, chain_in, kept, swap_out, swap_in,
+    bias_ref, lengths_ref, positives_ref, hid, wf, act, sums, vecs, packed, pooled, select, spread, both, twice, part_scores, score_parts,
+    grads, grads_t, targets, row_targets, lgrad, part, chain_out, chain_in, kept, swap_out, swap_in,
     wide_out, wide_in, near_out, near_in, summed,
-    local_sem, w_send, w_recv, t_send, t_recv, v_send, v_recv, g_send, g_recv,
+    local_sem, w_send, w_recv, t_send, t_recv, u_send, u_recv, v_send, v_recv, g_send, g_recv,
     s_send, s_recv, d_send, d_recv, c_send, c_recv, y_send, y_recv,
 ):
     dp = lax.axis_index("dp")
     vocab = lax.axis_index("vocab")
     x, y, core = dp // 8, (dp // 2) % 4, dp % 2
     z, hi = vocab // 2, vocab % 2
-    xc = x * 2 + core
+    xc = core * 4 + x
 
     def dp_of(xx, yy, cc):
         return (xx * 4 + yy) * 2 + cc
@@ -70,7 +70,7 @@
 
     y_peers = [dp_of(x, (y + o) % 4, core) for o in range(1, 4)]
     xc_peers = [(xc + o) % 8 for o in range(1, 8)]
-    xc_dp = [dp_of(p // 2, y, p % 2) for p in xc_peers]
+    xc_dp = [dp_of(p % 4, y, p // 4) for p in xc_peers]
     vocab_peers = [(vocab + o) % 16 for o in range(1, 16)]
 
     barrier = pltpu.get_barrier_semaphore()
@@ -235,7 +235,7 @@
     tile = jnp.zeros((8, 128), F32)
     for j in range(2):
         k = positives_ref[j]
-        place = (k // 16) * 16 + ((k // 2) % 2) * 8 + ((k // 4) % 4) * 2 + k % 2
+        place = ((k // 2) % 2) * 32 + (k // 16) * 8 + ((k // 4) % 4) * 2 + k % 2
         tile = tile + jnp.where((trow == 2 * y + j) & (tcol == place), 1.0, 0.0)
     targets[y] = tile
 
@@ -248,6 +248,12 @@
     neighbours(1)
     column(3)
     rest_out()
+    for o in range(1, 4):
+        yy = (y + o) % 4
+        pltpu.make_async_copy(targets.at[yy], targets.at[yy], t_recv.at[yy]).wait()
+    row_targets[x] = targets[0] + targets[1] + targets[2] + targets[3]
+    for i, p in enumerate((right, left, far)):
+        remote(row_targets.at[x], row_targets.at[x], u_send.at[i], u_recv.at[x], dp_of(p, y, core), vocab)
     last(0)
     rest_last()
     neighbours(2)
@@ -261,8 +267,8 @@
     for t in range(4):
         dots(t)
     for o in range(1, 4):
-        yy = (y + o) % 4
-        pltpu.make_async_copy(targets.at[yy], targets.at[yy], t_recv.at[yy]).wait()
+        block = row_targets.at[(x + o) % 4]
+        pltpu.make_async_copy(block, block, u_recv.at[(x + o) % 4]).wait()
 
     def pool(b, carry):
         cols = pl.ds(pl.multiple_of(b * 128, 128), 128)
@@ -302,26 +308,30 @@
     flat = pooled[...].reshape(512, 256)
     for i in range(4):
         both[:, pl.ds(256 * i, 256)] = jnp.dot(select[i], flat, preferred_element_type=F32).astype(BF)
+    passages = both[pl.ds(0, PAIRS), :]
+    twice[pl.ds(0, PAIRS), :] = passages
+    twice[pl.ds(PAIRS, PAIRS), :] = passages
     nt = (((1,), (1,)), ((), ()))
-    part_scores[...] = lax.dot_general(both[pl.ds(PAIRS, PAIRS), :], both[...], nt, preferred_element_type=F32)
+    part_scores[...] = lax.dot_general(both[pl.ds(PAIRS, PAIRS), :], twice[...], nt, preferred_element_type=F32)
 
     rows8 = pl.ds(pl.multiple_of(xc * 8, 8), 8)
-    score_parts[vocab] = part_scores[rows8, :]
+    low_lanes = lax.broadcasted_iota(jnp.int32, (16, 128), 1) < PAIRS
+    first_rows = pl.ds(pl.multiple_of(core * 32, 16), 16)
+    next_rows = pl.ds(pl.multiple_of(core * 32 + 16, 16), 16)
+    score_parts[vocab] = jnp.where(low_lanes, part_scores[first_rows, :], part_scores[next_rows, :])
     for i, p in enumerate(vocab_peers):
         remote(score_parts.at[vocab], score_parts.at[vocab], s_send.at[i], s_recv.at[vocab], dp, p)
-    target = targets[0] + targets[1] + targets[2] + targets[3]
     for p in vocab_peers:
         pltpu.make_async_copy(score_parts.at[p], score_parts.at[p], s_recv.at[p]).wait()
-    scores = SCORE_SCALE * jnp.sum(score_parts[...], axis=0)
-    valid = tcol < PAIRS
+    summed_parts = jnp.sum(score_parts[...], axis=0)
+    scores = SCORE_SCALE * jnp.concatenate([summed_parts, pltpu.roll(summed_parts, PAIRS, 1)], axis=0)
+    valid = lax.broadcasted_iota(jnp.int32, (32, 128), 1) < PAIRS
     top = jnp.max(jnp.where(valid, scores, -jnp.inf), axis=1, keepdims=True)
     shifted = jnp.where(valid, jnp.exp(jnp.where(valid, scores - top, 0.0)), 0.0)
     soft = shifted / jnp.sum(shifted, axis=1, keepdims=True)
-    grads[pl.ds(xc, 1)] = (LOSS_SCALE * (soft - target)).reshape(1, 8, 128)
-    for i, p in enumerate(xc_dp):
-        remote(grads.at[xc], grads.at[xc], d_send.at[i], d_recv.at[xc], p, vocab)
-    for p in xc_peers:
-        pltpu.make_async_copy(grads.at[p], grads.at[p], d_recv.at[p]).wait()
+    grads[pl.ds(core, 1)] = (LOSS_SCALE * (soft - row_targets[...].reshape(32, 128))).reshape(1, 32, 128)
+    remote(grads.at[core], grads.at[core], d_send.at[0], d_recv.at[core], sibling, vocab)
+    pltpu.make_async_copy(grads.at[1 - core], grads.at[1 - core], d_recv.at[1 - core]).wait()
     whole = jnp.concatenate([grads[...].reshape(PAIRS, 128), jnp.zeros((PAIRS, 128), F32)], axis=0)
     grads_t[...] = whole.T
 
@@ -334,7 +344,8 @@
         out = out + jnp.dot(b, rhs, preferred_element_type=F32)
         return out + jnp.dot(a, rhs, preferred_element_type=F32)
 
-    q_grad = exact_dot(grads[pl.ds(xc, 1)].reshape(8, 128)[:, :PAIRS], both[pl.ds(0, PAIRS), :])
+    rows8_here = pl.ds(pl.multiple_of(x * 8, 8), 8)
+    q_grad = exact_dot(grads[core, rows8_here, :][:, :PAIRS], both[pl.ds(0, PAIRS), :])
     p_grad = exact_dot(grads_t[rows8, :][:, :PAIRS], both[pl.ds(PAIRS, PAIRS), :])
     srow = lax.broadcasted_iota(jnp.int32, (8, SLICE), 0)
     for n, (start, size) in enumerate(SEGMENTS):
@@ -471,10 +482,12 @@
             vmem((4, 128, 512), BF),
             vmem((256, 256), BF),
             vmem((128, SLICE), BF),
+            vmem((128, SLICE), BF),
             vmem((PAIRS, 128), F32),
-            vmem((16, 8, 128), F32),
-            vmem((8, 8, 128), F32),
+            vmem((16, 16, 128), F32),
+            vmem((2, 32, 128), F32),
             vmem((128, 128), F32),
+            vmem((4, 8, 128), F32),
             vmem((4, 8, 128), F32),
             vmem((256, SLICE), BF),
             vmem((256, WIDTH), F32),
@@ -492,9 +505,10 @@
             dma((128,)), dma((96,)),
             dma((3,)), dma((4,)),
             dma((3,)), dma((4,)),
+            dma((3,)), dma((4,)),
             dma((7,)), dma((8,)),
             dma((15,)), dma((16,)),
-            dma((7,)), dma((8,)),
+            dma((1,)), dma((2,)),
             dma((STREAMS, 7)), dma((STREAMS, 7)),
             dma((STREAMS,)), dma((STREAMS,)),
         ],

time: 112 us -> 110 us (0.982)
  Pallas kernels: 111 us -> 108 us
    pallas_call x1, Pallas kernels: 111 us -> 108 us  [per_device(): pl.pallas_call(kernel, out_shape=jax.ShapeDtypeStruct((OWN, WIDTH), BF),...]
where the time goes in v3:
time: 110 us; the launch traced here: 109 us
  Pallas kernels  108 us (98%)
  local copies, waits for them, and re-layouts  1.57 us (1%)
    pallas_call x1, Pallas kernels, per_device(): pl.pallas_call(kernel, out_shape=jax.ShapeDtypeStruct((OWN, WIDTH), BF),...  108 us

profile of v3, /device:TPU:1, one launch (start us, length us, event | category | flops | bytes accessed | tf_op | source)
XLA Modules:
  0.0 109.4 jit_solution(4740265691736671384)
XLA Ops:
  0.0 107.8 %shard_map.55 = bf16[14,4096]{1,0:T(8,128)(2,1)} custom-call(bf16[224,4096]{1,0:T(8,128)(2,1)} %hidden_ref.1, bf16[128,1024]{1,0:T(8,128)(2,1)} %weight_ref.1, f32[1,1024]{1,0:T(1,128)} %bitcast.1, s32[2,2]{1,0:T(2,128)} %lengths_hbm.1, s32[2]{0:T(128)} %positives_hbm.1), custom_call_target="tpu_custom_call" | custom-call | flops 3758096384 | bytes 4194304 | tf_op jit(solution)/shard_map/pallas_call | solution.py:460
  107.8 1.6 %copy.7 = bf16[14,4096]{1,0:T(8,128)(2,1)} copy(bf16[14,4096]{1,0:T(8,128)(2,1)} %shard_map.55) | data formatting | bytes 229376

commit v4 on v3

--- a/solution.py
+++ b/solution.py
@@ -45,7 +45,7 @@
     grads, grads_t, targets, row_targets, lgrad, part, chain_out, chain_in, kept, swap_out, swap_in,
     wide_out, wide_in, near_out, near_in, summed,
     local_sem, w_send, w_recv, t_send, t_recv, u_send, u_recv, v_send, v_recv, g_send, g_recv,
-    s_send, s_recv, d_send, d_recv, c_send, c_recv, y_send, y_recv,
+    s_send, s_recv, d_send, d_recv, c_send, c_recv, y_send, y_recv, plane_sem, vocab_sem, last_sem,
 ):
     dp = lax.axis_index("dp")
     vocab = lax.axis_index("vocab")
@@ -73,14 +73,59 @@
     xc_dp = [dp_of(p % 4, y, p // 4) for p in xc_peers]
     vocab_peers = [(vocab + o) % 16 for o in range(1, 16)]
 
+    right, left, far = (x + 1) % 4, (x + 3) % 4, (x + 2) % 4
+    to_right, to_left = dp_of(right, y, core), dp_of(left, y, core)
+    above, below = dp_of(x, jnp.minimum(y + 1, 3), core), dp_of(x, jnp.maximum(y - 1, 0), core)
+    sibling = dp_of(x, y, 1 - core)
+    white = (x + y + core + z + hi) % 2 == 1
+    black = jnp.logical_not(white)
+    others = [((z + o) % 8) * 2 + (1 - hi if o % 2 == 0 else hi) for o in range(8)]
+    plane_count = jnp.where((y == 0) | (y == 3), 4, 5)
     barrier = pltpu.get_barrier_semaphore()
-    for p in y_peers + xc_dp:
-        pl.semaphore_signal(barrier, inc=1, device_id={"dp": p, "vocab": vocab}, device_id_type=MESH)
-    for p in vocab_peers:
-        pl.semaphore_signal(barrier, inc=1, device_id={"dp": dp, "vocab": p}, device_id_type=MESH)
+
+    def greet(sem, to_dp, to_vocab):
+        pl.semaphore_signal(sem, inc=1, device_id={"dp": to_dp, "vocab": to_vocab}, device_id_type=MESH)
+
+    def greet_plane(sem):
+        for p in (to_right, to_left, sibling):
+            greet(sem, p, vocab)
+        pl.when(y < 3)(lambda: greet(sem, above, vocab))
+        pl.when(y > 0)(lambda: greet(sem, below, vocab))
+
+    def greet_others(sem):
+        for p in others:
+            greet(sem, dp, p)
+
+    pl.when(white)(lambda: greet_plane(barrier))
+    pl.when(black)(lambda: greet_others(barrier))
+
+    @pl.when(black)
+    def _():
+        pl.semaphore_wait(barrier, plane_count)
+        greet_plane(plane_sem)
+
+    @pl.when(white)
+    def _():
+        pl.semaphore_wait(plane_sem, plane_count)
+
+    def others_answer():
+        @pl.when(white)
+        def _():
+            pl.semaphore_wait(barrier, 8)
+            greet_others(vocab_sem)
+
+    def others_known():
+        @pl.when(black)
+        def _():
+            pl.semaphore_wait(vocab_sem, 8)
+            greet(last_sem, dp, z * 2 + 1 - hi)
+
+    def all_known():
+        @pl.when(white)
+        def _():
+            pl.semaphore_wait(last_sem, 1)
 
     load_w.wait()
-    pl.semaphore_wait(barrier, 25)
 
     sends = []
     copies = []
@@ -121,11 +166,6 @@
             pl.when(cond)(copy.start)
         sends.append((cond, copy))
 
-    right, left, far = (x + 1) % 4, (x + 3) % 4, (x + 2) % 4
-    to_right, to_left = dp_of(right, y, core), dp_of(left, y, core)
-    above, below = dp_of(x, jnp.minimum(y + 1, 3), core), dp_of(x, jnp.maximum(y - 1, 0), core)
-    sibling = dp_of(x, y, 1 - core)
-
     def line_place(t):
         low = jnp.where(y < 2, y, 3 - y)
         place = jnp.where((low == 1) & (t < 2), 1 - t, t)
@@ -239,21 +279,16 @@
         tile = tile + jnp.where((trow == 2 * y + j) & (tcol == place), 1.0, 0.0)
     targets[y] = tile
 
-    for i, p in enumerate(y_peers):
-        remote(targets.at[y], targets.at[y], t_send.at[i], t_recv.at[y], p, vocab)
     column(1)
     neighbours(0)
     column(2)
     rest_neighbours()
     neighbours(1)
+    others_answer()
     column(3)
     rest_out()
-    for o in range(1, 4):
-        yy = (y + o) % 4
-        pltpu.make_async_copy(targets.at[yy], targets.at[yy], t_recv.at[yy]).wait()
-    row_targets[x] = targets[0] + targets[1] + targets[2] + targets[3]
-    for i, p in enumerate((right, left, far)):
-        remote(row_targets.at[x], row_targets.at[x], u_send.at[i], u_recv.at[x], dp_of(p, y, core), vocab)
+    for i, p in enumerate(y_peers):
+        remote(targets.at[y], targets.at[y], t_send.at[i], t_recv.at[y], p, vocab)
     last(0)
     rest_last()
     neighbours(2)
@@ -262,8 +297,15 @@
     neighbours(3)
     rest_line(2)
     last(2)
+    for o in range(1, 4):
+        yy = (y + o) % 4
+        pltpu.make_async_copy(targets.at[yy], targets.at[yy], t_recv.at[yy]).wait()
+    row_targets[x] = targets[0] + targets[1] + targets[2] + targets[3]
+    for i, p in enumerate((right, left, far)):
+        remote(row_targets.at[x], row_targets.at[x], u_send.at[i], u_recv.at[x], dp_of(p, y, core), vocab)
     rest_line(3)
     last(3)
+    others_known()
     for t in range(4):
         dots(t)
     for o in range(1, 4):
@@ -319,6 +361,7 @@
     first_rows = pl.ds(pl.multiple_of(core * 32, 16), 16)
     next_rows = pl.ds(pl.multiple_of(core * 32 + 16, 16), 16)
     score_parts[vocab] = jnp.where(low_lanes, part_scores[first_rows, :], part_scores[next_rows, :])
+    all_known()
     for i, p in enumerate(vocab_peers):
         remote(score_parts.at[vocab], score_parts.at[vocab], s_send.at[i], s_recv.at[vocab], dp, p)
     for p in vocab_peers:
@@ -511,6 +554,7 @@
             dma((1,)), dma((2,)),
             dma((STREAMS, 7)), dma((STREAMS, 7)),
             dma((STREAMS,)), dma((STREAMS,)),
+            pltpu.SemaphoreType.REGULAR, pltpu.SemaphoreType.REGULAR, pltpu.SemaphoreType.REGULAR,
         ],
         compiler_params=pltpu.CompilerParams(
             collective_id=0, has_side_effects=True, vmem_limit_bytes=63 * 1024 * 1024

time: 110 us -> 105 us (0.955)
  Pallas kernels: 108 us -> 102 us
    pallas_call x1, Pallas kernels: 108 us -> 102 us  [per_device(): pl.pallas_call(kernel, out_shape=jax.ShapeDtypeStruct((OWN, WIDTH), BF),...]
where the time goes in v4:
time: 105 us; the launch traced here: 104 us
  Pallas kernels  102 us (97%)
  local copies, waits for them, and re-layouts  1.57 us (1%)
    pallas_call x1, Pallas kernels, per_device(): pl.pallas_call(kernel, out_shape=jax.ShapeDtypeStruct((OWN, WIDTH), BF),...  102 us

profile of v4, /device:TPU:1, one launch (start us, length us, event | category | flops | bytes accessed | tf_op | source)
XLA Modules:
  0.0 103.8 jit_solution(13854042251490999402)
XLA Ops:
  0.0 102.2 %shard_map.55 = bf16[14,4096]{1,0:T(8,128)(2,1)} custom-call(bf16[224,4096]{1,0:T(8,128)(2,1)} %hidden_ref.1, bf16[128,1024]{1,0:T(8,128)(2,1)} %weight_ref.1, f32[1,1024]{1,0:T(1,128)} %bitcast.1, s32[2,2]{1,0:T(2,128)} %lengths_hbm.1, s32[2]{0:T(128)} %positives_hbm.1), custom_call_target="tpu_custom_call" | custom-call | flops 3758096384 | bytes 4194304 | tf_op jit(solution)/shard_map/pallas_call | solution.py:503
  102.2 1.6 %copy.7 = bf16[14,4096]{1,0:T(8,128)(2,1)} copy(bf16[14,4096]{1,0:T(8,128)(2,1)} %shard_map.55) | data formatting | bytes 229376

commit v5 on v4

--- a/solution.py
+++ b/solution.py
@@ -284,13 +284,13 @@
     column(2)
     rest_neighbours()
     neighbours(1)
-    others_answer()
     column(3)
     rest_out()
     for i, p in enumerate(y_peers):
         remote(targets.at[y], targets.at[y], t_send.at[i], t_recv.at[y], p, vocab)
     last(0)
     rest_last()
+    others_answer()
     neighbours(2)
     rest_line(1)
     last(1)
@@ -303,11 +303,13 @@
     row_targets[x] = targets[0] + targets[1] + targets[2] + targets[3]
     for i, p in enumerate((right, left, far)):
         remote(row_targets.at[x], row_targets.at[x], u_send.at[i], u_recv.at[x], dp_of(p, y, core), vocab)
+    dots(0)
+    dots(1)
     rest_line(3)
     last(3)
     others_known()
-    for t in range(4):
-        dots(t)
+    dots(2)
+    dots(3)
     for o in range(1, 4):
         block = row_targets.at[(x + o) % 4]
         pltpu.make_async_copy(block, block, u_recv.at[(x + o) % 4]).wait()

time: 105 us -> 105 us (level)
  no operation moved by 1% of the time
where the time goes in v5:
time: 105 us; the launch traced here: 104 us
  Pallas kernels  102 us (97%)
  local copies, waits for them, and re-layouts  1.57 us (1%)
    pallas_call x1, Pallas kernels, per_device(): pl.pallas_call(kernel, out_shape=jax.ShapeDtypeStruct((OWN, WIDTH), BF),...  102 us

profile of v5, /device:TPU:1, one launch (start us, length us, event | category | flops | bytes accessed | tf_op | source)
XLA Modules:
  0.0 103.6 jit_solution(13552493201093224578)
XLA Ops:
  0.0 102.0 %shard_map.55 = bf16[14,4096]{1,0:T(8,128)(2,1)} custom-call(bf16[224,4096]{1,0:T(8,128)(2,1)} %hidden_ref.1, bf16[128,1024]{1,0:T(8,128)(2,1)} %weight_ref.1, f32[1,1024]{1,0:T(1,128)} %bitcast.1, s32[2,2]{1,0:T(2,128)} %lengths_hbm.1, s32[2]{0:T(128)} %positives_hbm.1), custom_call_target="tpu_custom_call" | custom-call | flops 3758096384 | bytes 4194304 | tf_op jit(solution)/shard_map/pallas_call | solution.py:505
  102.1 1.6 %copy.7 = bf16[14,4096]{1,0:T(8,128)(2,1)} copy(bf16[14,4096]{1,0:T(8,128)(2,1)} %shard_map.55) | data formatting | bytes 229376
